TPU v7x, 256 devices: a whole 4x4x8 slice. The times are simulated.
256 devices in a mesh: wide: 16 (over x, y_lo, core), narrow: 16 (over y_hi, z).
Axes of the slice: x: 4, y: 4 (y_hi: 2, y_lo: 2; y = y_hi * 2 + y_lo), z: 8, core: 2. Of those that a mesh axis runs over, the one named last changes fastest.
Arguments:
- pose_feats: bfloat16 [16384, 1024], P(('wide', 'narrow')), may hold values from -3 to 3
- text_feats: bfloat16 [16384, 1024], P(('wide', 'narrow')), may hold values from -3 to 3
- match: int32 [16384], P(('wide', 'narrow')), may hold values from 0 to 16383, as said below
- pose_head: bfloat16 [1024, 1024], replicated, may hold values from -1 to 1
- text_head: bfloat16 [1024, 1024], replicated, may hold values from -1 to 1
Outputs:
- loss: float32 [], replicated
- grad_pose: float32 [16384, 1024], P(('wide', 'narrow'))
- grad_text: float32 [16384, 1024], P(('wide', 'narrow'))
- head_grads: float32 [1024, 2048], P('wide')
Inputs may be any that keep to these rules, and one draw needn't show every extreme that they name: `match`: every text index appears exactly once.
All inputs are finite; a program needn't handle non-finite values.
Results may differ from a plain program's by a relative error of at most 0.0049.
Values may be sent and summed in bfloat16 or wider, within the bound.
No kernel may reach another device: no remote copies, remote signals or barrier semaphores. Data moves between devices by JAX's collectives and lax.ppermute only.
A program may use at most 64 MiB of HBM per device.

v0:
```python
import math

import jax
import jax.numpy as jnp
from jax import lax
from jax.sharding import PartitionSpec as P

epsilon = 1e-06
logit_bias = -10.0


def from_behind(value, axis, by):
    count = lax.axis_size(axis)
    return lax.ppermute(value, axis, [(i, (i + by) % count) for i in range(count)])


def unit_rows(raw_rows):
    norm_rows = jnp.sqrt(jnp.sum(raw_rows * raw_rows, axis=1, keepdims=True) + epsilon)
    return (raw_rows / norm_rows, norm_rows)


def back_rows(grad_rows, unit_vals, norm_rows):
    inner_part = jnp.sum(unit_vals * grad_rows, axis=1, keepdims=True)
    return ((grad_rows - unit_vals * inner_part) / norm_rows).astype(jnp.bfloat16)


def advance(text_block):
    return from_behind(text_block, "wide", 1)


def return_grad(text_acc):
    return from_behind(text_acc, "wide", 1)


def local(pose_feats, text_feats, match, pose_head, text_head):
    row_count = pose_feats.shape[0]
    embed_width = pose_head.shape[1]
    n_wide = lax.axis_size("wide")
    n_narrow = lax.axis_size("narrow")
    batch_size = row_count * n_wide * n_narrow
    logit_scale = 2.0 * math.sqrt(embed_width)
    grad_scale = logit_scale / math.sqrt(batch_size)
    pose_unit, pose_norm = unit_rows(
        jnp.dot(pose_feats, pose_head, preferred_element_type=jnp.float32)
    )
    text_unit, text_norm = unit_rows(
        jnp.dot(text_feats, text_head, preferred_element_type=jnp.float32)
    )
    pose_embed = pose_unit.astype(jnp.bfloat16)
    text_embed = text_unit.astype(jnp.bfloat16)
    pose_group = lax.all_gather(pose_embed, "narrow", axis=0, tiled=True)
    group_ids = lax.all_gather(match, "narrow", axis=0, tiled=True)
    wide_index = lax.axis_index("wide")
    narrow_index = lax.axis_index("narrow")
    local_ids = jnp.arange(row_count, dtype=jnp.int32)

    def score_block(text_block, anchor):
        text_ids = (anchor * n_narrow + narrow_index) * row_count + local_ids
        logits = (
            logit_scale
            * lax.dot_general(
                text_block, pose_group, (((1,), (1,)), ((), ())), preferred_element_type=jnp.float32
            )
            + logit_bias
        )
        pair_sign = jnp.where(group_ids[None, :] == text_ids[:, None], 1.0, -1.0).astype(
            jnp.float32
        )
        loss_part = jnp.sum(jax.nn.softplus(-pair_sign * logits))
        weights = (-pair_sign * jax.nn.sigmoid(-pair_sign * logits) * grad_scale).astype(
            jnp.bfloat16
        )
        pose_part = lax.dot_general(
            weights, text_block, (((0,), (0,)), ((), ())), preferred_element_type=jnp.float32
        )
        text_part = jnp.dot(weights, pose_group, preferred_element_type=jnp.float32)
        return (loss_part, pose_part, text_part)

    own_loss, own_pose, own_text = score_block(text_embed, wide_index)

    def carry_step(step_index, state):
        loss_total, pose_grad, text_block, text_acc = state
        text_acc = return_grad(text_acc)
        text_block = advance(text_block)
        loss_part, pose_part, text_part = score_block(
            text_block, (wide_index - step_index) % n_wide
        )
        return (loss_total + loss_part, pose_grad + pose_part, text_block, text_acc + text_part)

    loss_total, pose_grad, text_block, text_acc = lax.fori_loop(
        1, n_wide, carry_step, (own_loss, own_pose, text_embed, own_text)
    )
    text_grad = return_grad(text_acc)
    pose_own = lax.psum_scatter(pose_grad, "narrow", scatter_dimension=0, tiled=True)
    loss_all = lax.psum(loss_total, ("wide", "narrow"))
    loss = loss_all / (batch_size * batch_size)
    pose_back = back_rows(pose_own, pose_unit, pose_norm)
    text_back = back_rows(text_grad, text_unit, text_norm)
    grad_pose = lax.dot_general(
        pose_back, pose_head, (((1,), (1,)), ((), ())), preferred_element_type=jnp.float32
    )
    grad_text = lax.dot_general(
        text_back, text_head, (((1,), (1,)), ((), ())), preferred_element_type=jnp.float32
    )
    pose_term = lax.dot_general(
        pose_feats, pose_back, (((0,), (0,)), ((), ())), preferred_element_type=jnp.float32
    )
    text_term = lax.dot_general(
        text_feats, text_back, (((0,), (0,)), ((), ())), preferred_element_type=jnp.float32
    )
    head_part = lax.psum_scatter(
        jnp.concatenate([pose_term, text_term], axis=1), "wide", scatter_dimension=0, tiled=True
    )
    head_grads = lax.psum(head_part, "narrow")
    return (loss, grad_pose, grad_text, head_grads)


def solution(mesh):
    placed = (
        P(("wide", "narrow"), None),
        P(("wide", "narrow"), None),
        P(("wide", "narrow")),
        P(),
        P(),
    )
    return jax.shard_map(
        local,
        mesh=mesh,
        in_specs=placed,
        out_specs=(P(), P(("wide", "narrow"), None), P(("wide", "narrow"), None), P("wide", None)),
        check_vma=False,
    )
```

profile of v0, /device:TPU:32, one launch (start us, length us, event | category | flops | bytes accessed | tf_op | source)
XLA Modules:
  0.0 864.2 jit_solution(10955186972601229227)
XLA Ops:
  7.3 2.4 multiply_reduce_fusion.2
  12.1 20.0 %all-reduce = s32[1024]{0:T(1024)S(1)} all-reduce(s32[1024]{0:T(1024)S(1)} %dynamic-update-slice), channel_id=1, replica_groups=mesh['wide'=16,'narrow'=16] {'narrow'}, use_global_device_ids=true, to_apply=%add | all-reduce | flops 1024 | bytes 8192
  32.9 65.9 %all-gather.2.cloned.1.call-done = bf16[1024,1024]{1,0:T(8,128)(2,1)} async-done(((bf16[64,1024]{1,0:T(8,128)(2,1)}), bf16[1024,1024]{1,0:T(8,128)(2,1)}) %all-gather.2.cloned.1.call-update) | async-done | bytes 2097168 | tf_op jit(solution)/shard_map/all_gather | solution.py:51
  98.8 3.1 fusion.7
  101.9 2.7 fusion.11
  105.9 265.6 %while.22 = (s32[]{:T(128)}, f32[]{:T(128)}, f32[1024,1024]{1,0:T(8,128)}, bf16[64,1024]{1,0:T(8,128)(2,1)S(1)}, f32[64,1024]{1,0:T(8,128)}, /*index=5*/s32[1024...) while((s32[]{:T(128)}, f32[]{:T(128)}, ...), condition=%wide.region_5.6_spmd.clone, body=%wide.region_3.5_spmd.clone.sunk | while | flops 405798976 | bytes 24393120 | solution.py:90
  106.6 5.8 collective-permute-done
  112.4 3.1 fusion.39
  116.7 5.1 convolution_add_fusion.4
  123.6 6.5 collective-permute-done
  130.1 3.1 fusion.39
  134.4 5.1 convolution_add_fusion.4
  141.3 6.5 collective-permute-done
  147.8 3.1 fusion.39
  152.1 5.1 convolution_add_fusion.4
  159.0 6.5 collective-permute-done
  165.5 3.1 fusion.39
  169.9 5.1 convolution_add_fusion.4
  176.7 6.5 collective-permute-done
  183.2 3.1 fusion.39
  187.6 5.1 convolution_add_fusion.4
  194.4 6.5 collective-permute-done
  200.9 3.1 fusion.39
  205.3 5.1 convolution_add_fusion.4
  212.1 6.5 collective-permute-done
  218.6 3.1 fusion.39
  223.0 5.1 convolution_add_fusion.4
  229.9 6.5 collective-permute-done
  236.3 3.1 fusion.39
  240.7 5.1 convolution_add_fusion.4
  247.6 6.5 collective-permute-done
  254.1 3.1 fusion.39
  258.4 5.1 convolution_add_fusion.4
  265.3 6.5 collective-permute-done
  271.8 3.1 fusion.39
  276.1 5.1 convolution_add_fusion.4
  283.0 6.5 collective-permute-done
  289.5 3.1 fusion.39
  293.8 5.1 convolution_add_fusion.4
  300.7 6.5 collective-permute-done
  307.2 3.1 fusion.39
  311.5 5.1 convolution_add_fusion.4
  318.4 6.5 collective-permute-done
  324.9 3.1 fusion.39
  329.2 5.1 convolution_add_fusion.4
  336.1 6.5 collective-permute-done
  342.6 3.1 fusion.39
  347.0 5.1 convolution_add_fusion.4
  353.8 6.5 collective-permute-done
  360.3 3.1 fusion.39
  364.7 5.1 convolution_add_fusion.4
  371.7 8.1 collective-permute-done.2
  380.0 2.8 convolution_bitcast_fusion
  382.8 194.3 %reduce-scatter.5.cloned.1.call-done = f32[64,1024]{1,0:T(8,128)} async-done(((f32[1024,1024]{1,0:T(8,128)}), f32[64,1024]{1,0:T(8,128)}) %reduce-scatter.5.cloned.1.call-update) | async-done | bytes 262160 | tf_op jit(solution)/shard_map/reduce_scatter | solution.py:94
  578.3 1.9 convolution_bitcast_fusion.1
  580.5 4.1 pad_maximum_fusion
  584.6 9.1 %copy.11 = f32[1024,2048]{1,0:T(8,128)} copy(f32[1024,2048]{0,1:T(8,128)} %pad_maximum_fusion) | data formatting | bytes 16777216
  593.8 78.3 %psum.14 = f32[]{:T(128)} all-reduce(f32[]{:T(128)} %get-tuple-element.249), channel_id=1, replica_groups=mesh['wide'=16,'narrow'=16] {'wide','narrow'}, use_global_device_ids=true, to_apply=%region_6.7 | all-reduce | flops 1 | bytes 8 | tf_op jit(solution)/shard_map/psum | solution.py:95
  672.8 18.6 %reduce-scatter.7.cloned.1.call-done = f32[64,2048]{1,0:T(8,128)} async-done(((f32[1024,2048]{1,0:T(8,128)}), f32[64,2048]{1,0:T(8,128)}) %reduce-scatter.7.cloned.1.call-update) | async-done | bytes 524304
  691.4 2.4 copy.12
  693.8 1.5 fusion.13
  695.5 1.5 fusion.12
  697.0 157.3 %all-reduce.3.cloned.1.call-done = f32[64,2048]{0,1:T(8,128)} async-done(((f32[64,2048]{0,1:T(8,128)}), f32[64,2048]{0,1:T(8,128)}) %all-reduce.3.cloned.1.call-update) | async-done | bytes 524304 | tf_op jit(solution)/shard_map/psum | solution.py:114
  854.2 2.3 copy.10
  (159 shorter events, 25.6 us)
Async XLA Ops:
  7.2 25.0 %copy-start = (bf16[1024,1024]{1,0:T(8,128)(2,1)S(1)}, bf16[1024,1024]{1,0:T(8,128)(2,1)}, u32[]{:S(2)}) copy-start(bf16[1024,1024]{1,0:T(8,128)(2,1)} %param.11) | copy-start | bytes 6291460
  7.2 3.3 copy-start.9
  7.2 4.7 copy-start.8
  7.2 25.0 %copy-start.4 = (bf16[64,1024]{1,0:T(8,128)(2,1)S(1)}, bf16[64,1024]{1,0:T(8,128)(2,1)}, u32[]{:S(2)}) copy-start(bf16[64,1024]{1,0:T(8,128)(2,1)} %param.8) | copy-start | bytes 393220
  7.2 91.6 %all-gather.2.cloned.1.call-start = ((), (), s32[]{:S(2)}) async-start(), calls=%async_computation.2 | async-start | bytes 2228224 | tf_op jit(solution)/shard_map/all_gather | solution.py:51
  10.4 566.7 %reduce-scatter.5.cloned.1.call-start = ((), (), s32[]{:S(2)}) async-start(), calls=%async_computation.3 | async-start | bytes 4456448 | tf_op jit(solution)/shard_map/reduce_scatter | solution.py:94
  101.9 2.7 copy-start.6
  105.9 6.5 collective-permute-start
  105.9 15.9 %collective-permute-start.1 = (f32[64,1024]{1,0:T(8,128)}, f32[64,1024]{1,0:T(8,128)S(1)}, u32[]{:S(2)}, u32[]{:S(2)}) collective-permute-start(f32[64,1024]{1,0:T(8,128)} %get-tuple-element.383), channel_id=1, source_target_pairs={{0,16},{16,32},{32,48},{48,64},{64,80},{80,96},{96,112},{112,128},... | collective-permute-start | bytes 786440 | tf_op jit(solution)/shard_map/while/body/eval_jaxpr/ppermute | solution.py:14
  116.7 5.1 copy-start.7
  123.6 6.5 collective-permute-start
  123.6 15.9 %collective-permute-start.1 = (f32[64,1024]{1,0:T(8,128)}, f32[64,1024]{1,0:T(8,128)S(1)}, u32[]{:S(2)}, u32[]{:S(2)}) collective-permute-start(f32[64,1024]{1,0:T(8,128)} %get-tuple-element.383), channel_id=1, source_target_pairs={{0,16},{16,32},{32,48},{48,64},{64,80},{80,96},{96,112},{112,128},... | collective-permute-start | bytes 786440 | tf_op jit(solution)/shard_map/while/body/eval_jaxpr/ppermute | solution.py:14
  134.4 5.1 copy-start.7
  141.3 6.5 collective-permute-start
  141.3 15.9 %collective-permute-start.1 = (f32[64,1024]{1,0:T(8,128)}, f32[64,1024]{1,0:T(8,128)S(1)}, u32[]{:S(2)}, u32[]{:S(2)}) collective-permute-start(f32[64,1024]{1,0:T(8,128)} %get-tuple-element.383), channel_id=1, source_target_pairs={{0,16},{16,32},{32,48},{48,64},{64,80},{80,96},{96,112},{112,128},... | collective-permute-start | bytes 786440 | tf_op jit(solution)/shard_map/while/body/eval_jaxpr/ppermute | solution.py:14
  152.1 5.1 copy-start.7
  159.0 6.5 collective-permute-start
  159.0 15.9 %collective-permute-start.1 = (f32[64,1024]{1,0:T(8,128)}, f32[64,1024]{1,0:T(8,128)S(1)}, u32[]{:S(2)}, u32[]{:S(2)}) collective-permute-start(f32[64,1024]{1,0:T(8,128)} %get-tuple-element.383), channel_id=1, source_target_pairs={{0,16},{16,32},{32,48},{48,64},{64,80},{80,96},{96,112},{112,128},... | collective-permute-start | bytes 786440 | tf_op jit(solution)/shard_map/while/body/eval_jaxpr/ppermute | solution.py:14
  169.8 5.1 copy-start.7
  176.7 6.5 collective-permute-start
  176.7 15.9 %collective-permute-start.1 = (f32[64,1024]{1,0:T(8,128)}, f32[64,1024]{1,0:T(8,128)S(1)}, u32[]{:S(2)}, u32[]{:S(2)}) collective-permute-start(f32[64,1024]{1,0:T(8,128)} %get-tuple-element.383), channel_id=1, source_target_pairs={{0,16},{16,32},{32,48},{48,64},{64,80},{80,96},{96,112},{112,128},... | collective-permute-start | bytes 786440 | tf_op jit(solution)/shard_map/while/body/eval_jaxpr/ppermute | solution.py:14
  187.6 5.1 copy-start.7
  194.4 6.5 collective-permute-start
  194.4 15.9 %collective-permute-start.1 = (f32[64,1024]{1,0:T(8,128)}, f32[64,1024]{1,0:T(8,128)S(1)}, u32[]{:S(2)}, u32[]{:S(2)}) collective-permute-start(f32[64,1024]{1,0:T(8,128)} %get-tuple-element.383), channel_id=1, source_target_pairs={{0,16},{16,32},{32,48},{48,64},{64,80},{80,96},{96,112},{112,128},... | collective-permute-start | bytes 786440 | tf_op jit(solution)/shard_map/while/body/eval_jaxpr/ppermute | solution.py:14
  205.3 5.1 copy-start.7
  212.1 6.5 collective-permute-start
  212.1 15.9 %collective-permute-start.1 = (f32[64,1024]{1,0:T(8,128)}, f32[64,1024]{1,0:T(8,128)S(1)}, u32[]{:S(2)}, u32[]{:S(2)}) collective-permute-start(f32[64,1024]{1,0:T(8,128)} %get-tuple-element.383), channel_id=1, source_target_pairs={{0,16},{16,32},{32,48},{48,64},{64,80},{80,96},{96,112},{112,128},... | collective-permute-start | bytes 786440 | tf_op jit(solution)/shard_map/while/body/eval_jaxpr/ppermute | solution.py:14
  223.0 5.1 copy-start.7
  229.8 6.5 collective-permute-start
  229.8 15.9 %collective-permute-start.1 = (f32[64,1024]{1,0:T(8,128)}, f32[64,1024]{1,0:T(8,128)S(1)}, u32[]{:S(2)}, u32[]{:S(2)}) collective-permute-start(f32[64,1024]{1,0:T(8,128)} %get-tuple-element.383), channel_id=1, source_target_pairs={{0,16},{16,32},{32,48},{48,64},{64,80},{80,96},{96,112},{112,128},... | collective-permute-start | bytes 786440 | tf_op jit(solution)/shard_map/while/body/eval_jaxpr/ppermute | solution.py:14
  240.7 5.1 copy-start.7
  247.6 6.5 collective-permute-start
  247.6 15.9 %collective-permute-start.1 = (f32[64,1024]{1,0:T(8,128)}, f32[64,1024]{1,0:T(8,128)S(1)}, u32[]{:S(2)}, u32[]{:S(2)}) collective-permute-start(f32[64,1024]{1,0:T(8,128)} %get-tuple-element.383), channel_id=1, source_target_pairs={{0,16},{16,32},{32,48},{48,64},{64,80},{80,96},{96,112},{112,128},... | collective-permute-start | bytes 786440 | tf_op jit(solution)/shard_map/while/body/eval_jaxpr/ppermute | solution.py:14
  258.4 5.1 copy-start.7
  265.3 6.5 collective-permute-start
  265.3 15.9 %collective-permute-start.1 = (f32[64,1024]{1,0:T(8,128)}, f32[64,1024]{1,0:T(8,128)S(1)}, u32[]{:S(2)}, u32[]{:S(2)}) collective-permute-start(f32[64,1024]{1,0:T(8,128)} %get-tuple-element.383), channel_id=1, source_target_pairs={{0,16},{16,32},{32,48},{48,64},{64,80},{80,96},{96,112},{112,128},... | collective-permute-start | bytes 786440 | tf_op jit(solution)/shard_map/while/body/eval_jaxpr/ppermute | solution.py:14
  276.1 5.1 copy-start.7
  283.0 6.5 collective-permute-start
  283.0 15.9 %collective-permute-start.1 = (f32[64,1024]{1,0:T(8,128)}, f32[64,1024]{1,0:T(8,128)S(1)}, u32[]{:S(2)}, u32[]{:S(2)}) collective-permute-start(f32[64,1024]{1,0:T(8,128)} %get-tuple-element.383), channel_id=1, source_target_pairs={{0,16},{16,32},{32,48},{48,64},{64,80},{80,96},{96,112},{112,128},... | collective-permute-start | bytes 786440 | tf_op jit(solution)/shard_map/while/body/eval_jaxpr/ppermute | solution.py:14
  293.8 5.1 copy-start.7
  300.7 6.5 collective-permute-start
  300.7 15.9 %collective-permute-start.1 = (f32[64,1024]{1,0:T(8,128)}, f32[64,1024]{1,0:T(8,128)S(1)}, u32[]{:S(2)}, u32[]{:S(2)}) collective-permute-start(f32[64,1024]{1,0:T(8,128)} %get-tuple-element.383), channel_id=1, source_target_pairs={{0,16},{16,32},{32,48},{48,64},{64,80},{80,96},{96,112},{112,128},... | collective-permute-start | bytes 786440 | tf_op jit(solution)/shard_map/while/body/eval_jaxpr/ppermute | solution.py:14
  311.5 5.1 copy-start.7
  318.4 6.5 collective-permute-start
  318.4 15.9 %collective-permute-start.1 = (f32[64,1024]{1,0:T(8,128)}, f32[64,1024]{1,0:T(8,128)S(1)}, u32[]{:S(2)}, u32[]{:S(2)}) collective-permute-start(f32[64,1024]{1,0:T(8,128)} %get-tuple-element.383), channel_id=1, source_target_pairs={{0,16},{16,32},{32,48},{48,64},{64,80},{80,96},{96,112},{112,128},... | collective-permute-start | bytes 786440 | tf_op jit(solution)/shard_map/while/body/eval_jaxpr/ppermute | solution.py:14
  329.2 5.1 copy-start.7
  336.1 6.5 collective-permute-start
  336.1 15.9 %collective-permute-start.1 = (f32[64,1024]{1,0:T(8,128)}, f32[64,1024]{1,0:T(8,128)S(1)}, u32[]{:S(2)}, u32[]{:S(2)}) collective-permute-start(f32[64,1024]{1,0:T(8,128)} %get-tuple-element.383), channel_id=1, source_target_pairs={{0,16},{16,32},{32,48},{48,64},{64,80},{80,96},{96,112},{112,128},... | collective-permute-start | bytes 786440 | tf_op jit(solution)/shard_map/while/body/eval_jaxpr/ppermute | solution.py:14
  346.9 5.1 copy-start.7
  353.8 6.5 collective-permute-start
  353.8 15.9 %collective-permute-start.1 = (f32[64,1024]{1,0:T(8,128)}, f32[64,1024]{1,0:T(8,128)S(1)}, u32[]{:S(2)}, u32[]{:S(2)}) collective-permute-start(f32[64,1024]{1,0:T(8,128)} %get-tuple-element.383), channel_id=1, source_target_pairs={{0,16},{16,32},{32,48},{48,64},{64,80},{80,96},{96,112},{112,128},... | collective-permute-start | bytes 786440 | tf_op jit(solution)/shard_map/while/body/eval_jaxpr/ppermute | solution.py:14
  364.7 5.1 copy-start.7
  371.5 319.9 %reduce-scatter.7.cloned.1.call-start = ((), (), s32[]{:S(2)}) async-start(), calls=%async_computation.5 | async-start | bytes 8912896
  371.6 8.2 collective-permute-start.2
  380.0 198.2 %copy-start.5 = (bf16[64,1024]{1,0:T(8,128)(2,1)S(1)}, bf16[64,1024]{1,0:T(8,128)(2,1)}, u32[]{:S(2)}) copy-start(bf16[64,1024]{1,0:T(8,128)(2,1)} %param.7) | copy-start | bytes 393220
  578.3 2.3 copy-start.1
  593.8 260.5 %all-reduce.3.cloned.1.call-start = ((), (), s32[]{:S(2)}) async-start(), calls=%async_computation.4 | async-start | bytes 2097152 | tf_op jit(solution)/shard_map/psum | solution.py:114
  693.8 1.5 copy-start.3
  693.8 1.7 copy-start.2
Sparse Core Ops, SparseCore 0:
  11.2 87.5 all-gather.1
  371.7 205.3 reduce-scatter.4
  593.9 97.4 reduce-scatter.6
  694.1 160.1 all-reduce.2
where the time goes:
time: 867 us; the launch traced here: 864 us
  waiting for transfers between devices  541 us (62%)
  matrix products  159 us (18%)
  blocking collectives  98.3 us (11%)
  loops' own time  26.5 us (3%)
  between operations  16.4 us (2%)
  local copies, waits for them, and re-layouts  15.5 us (2%)
    reduce_scatter x1, waiting for transfers between devices, local(): lax.psum_scatter(pose_grad, 'narrow', scatter_dimension=0, tiled=True)  194 us
    psum x1, waiting for transfers between devices, local(): head_grads = lax.psum(head_part, 'narrow')  157 us
    ppermute x31, waiting for transfers between devices, from_behind(): lax.ppermute(value, axis, [(i, (i + by) % count) for i in range(count)])  105 us
    dot_general x16, matrix products, score_block(): lax.dot_general(weights, text_block, (((0,), (0,)), ((), ())), preferred_...  78.8 us
    psum x1, blocking collectives, local(): loss_all = lax.psum(loss_total, ('wide', 'narrow'))  78.3 us
    all_gather x1, waiting for transfers between devices, local(): pose_group = lax.all_gather(pose_embed, 'narrow', axis=0, tiled=True)  65.9 us
    dot_general x16, matrix products, score_block(): lax.dot_general(text_block, pose_group, (((1,), (1,)), ((), ())), preferr...  49.8 us
    another operation x1, loops' own time, local(): lax.fori_loop(1, n_wide, carry_step, (own_loss, own_pose, text_embed, own...  26.5 us
  transfers between devices with their start and end apart: 35, of which 20 were waited for; matrix products, arithmetic and copies ran while one was open for 15% of the time, Pallas kernels for 0%

commit v1 on v0

v1 whole, which is shorter than its diff:
```python
import functools
import math

import jax
import jax.numpy as jnp
from jax import lax
from jax.experimental import pallas as pl
from jax.experimental.pallas import tpu as pltpu
from jax.sharding import Mesh
from jax.sharding import PartitionSpec as P

epsilon = 1e-06
logit_bias = -10.0

AXES = ("x", "yl", "core", "yh", "z")
PLANE = ("x", "yl", "yh")
LINE = ("core", "z")
NARROW = ("yh", "z")
NX, NY, NZ, NC = 4, 4, 8, 2
ROWS = 64
N = 1024
EXTRA = 128
TILE = 256

NT = (((1,), (1,)), ((), ()))
TN = (((0,), (0,)), ((), ()))
NN = (((1,), (0,)), ((), ()))


def device_index(x, y, z, c):
    return (((x * 2 + y % 2) * 2 + c) * 2 + y // 2) * NZ + z


def pairs_of(move):
    out = []
    for x in range(NX):
        for y in range(NY):
            for z in range(NZ):
                for c in range(NC):
                    x2, y2, z2, c2 = move(x, y, z, c)
                    out.append(
                        (device_index(x, y, z, c), device_index(x2 % NX, y2 % NY, z2 % NZ, c2 % NC))
                    )
    return out


def send(value, move):
    return lax.ppermute(value, AXES, pairs_of(move))


def swap_cores(value):
    return send(value, lambda x, y, z, c: (x, y, z, 1 - c))


def plane_step(first, by):
    def move(x, y, z, c):
        return (x + by, y, z, c) if (c == 0) == first else (x, y + by, z, c)

    return move


def ring_gather(shard, first, place):
    half = shard.shape[0] // 2
    below = send(shard, plane_step(first, 1))
    above = send(shard, plane_step(first, -1))
    far_low = send(below[:half], plane_step(first, 1))
    far_high = send(above[half:], plane_step(first, -1))
    rows = shard.shape[0]
    out = jnp.zeros((4 * rows, shard.shape[1]), shard.dtype)
    for value, offset, start in (
        (shard, 0, 0),
        (below, 3, 0),
        (above, 1, 0),
        (far_low, 2, 0),
        (far_high, 2, half),
    ):
        out = lax.dynamic_update_slice(out, value, ((place + offset) % 4 * rows + start, 0))
    return out


def project_kernel(feats_ref, head_ref, embed_ref, unit_ref, norm_ref):
    @pl.loop(0, N // TILE)
    def _(step):
        cols = pl.ds(pl.multiple_of(step * TILE, TILE), TILE)
        raw = lax.dot_general(
            head_ref[...], feats_ref[cols, :N], NT, preferred_element_type=jnp.float32
        )
        norm = jnp.sqrt(jnp.sum(raw * raw, axis=0, keepdims=True) + epsilon)
        unit = raw / norm
        unit_ref[:, cols] = unit
        embed_ref[:, cols] = unit.astype(jnp.bfloat16)
        norm_ref[:, cols] = jnp.broadcast_to(norm, (8, TILE))


def back_cols(grad, unit, norm):
    inner = jnp.sum(unit * grad, axis=0, keepdims=True)
    return ((grad - unit * inner) / norm).astype(jnp.bfloat16)


def pair_kernel(
    scale,
    grad_scale,
    feats_ref,
    head_ref,
    pose_ref,
    pose_unit_ref,
    pose_norm_ref,
    target_ref,
    loss_ref,
    pose_back_ref,
    text_back_ref,
    text_ref,
    weights_ref,
):
    loss_ref[...] = jnp.zeros_like(loss_ref)
    target = target_ref[0:1, :]

    @pl.loop(0, N // TILE)
    def _(step):
        start = pl.multiple_of(step * TILE, TILE)
        cols = pl.ds(start, TILE)
        raw = lax.dot_general(
            head_ref[...], feats_ref[cols, :], NT, preferred_element_type=jnp.float32
        )
        norm = jnp.sqrt(jnp.sum(raw * raw, axis=0, keepdims=True) + epsilon)
        unit = raw / norm
        text = unit.astype(jnp.bfloat16)
        text_ref[:, cols] = text
        logits = (
            scale * lax.dot_general(text, pose_ref[...], TN, preferred_element_type=jnp.float32)
            + logit_bias
        )
        ids = lax.broadcasted_iota(jnp.int32, (TILE, 1), 0) + start
        paired = ids == target
        arg = jnp.where(paired, -logits, logits)
        small = jnp.exp(-jnp.abs(arg))
        loss = jnp.maximum(arg, 0.0) + jnp.log1p(small)
        loss_ref[...] += jnp.sum(loss.reshape(TILE // 8, 8, N), axis=0)
        share = 1.0 / (1.0 + small)
        sig = jnp.where(arg >= 0.0, share, small * share)
        weights = (jnp.where(paired, -grad_scale, grad_scale) * sig).astype(jnp.bfloat16)
        weights_ref[cols, :] = weights
        text_grad = lax.dot_general(
            pose_ref[...], weights, NT, preferred_element_type=jnp.float32
        )
        text_back_ref[:, cols] = back_cols(text_grad, unit, norm)

    @pl.loop(0, N // TILE)
    def _(step):
        cols = pl.ds(pl.multiple_of(step * TILE, TILE), TILE)
        pose_grad = lax.dot_general(
            text_ref[...], weights_ref[:, cols], NN, preferred_element_type=jnp.float32
        )
        pose_back_ref[:, cols] = back_cols(
            pose_grad, pose_unit_ref[:, cols], pose_norm_ref[0:1, cols]
        )


VMEM = pl.BlockSpec(memory_space=pltpu.VMEM)
LIMIT = pltpu.CompilerParams(vmem_limit_bytes=48 * 1024 * 1024)


def project(feats, head_t):
    return pl.pallas_call(
        project_kernel,
        out_shape=(
            jax.ShapeDtypeStruct((N, N), jnp.bfloat16),
            jax.ShapeDtypeStruct((N, N), jnp.float32),
            jax.ShapeDtypeStruct((8, N), jnp.float32),
        ),
        in_specs=[VMEM] * 2,
        out_specs=(VMEM,) * 3,
        compiler_params=LIMIT,
        cost_estimate=pl.CostEstimate(flops=2 * N**3, bytes_accessed=12 * N * N, transcendentals=0),
    )(feats, head_t)


def score(scale, grad_scale, feats, head_t, pose, pose_unit, pose_norm, target):
    return pl.pallas_call(
        functools.partial(pair_kernel, scale, grad_scale),
        out_shape=(
            jax.ShapeDtypeStruct((8, N), jnp.float32),
            jax.ShapeDtypeStruct((N, N), jnp.bfloat16),
            jax.ShapeDtypeStruct((N, N), jnp.bfloat16),
        ),
        in_specs=[VMEM] * 6,
        out_specs=(VMEM,) * 3,
        scratch_shapes=[pltpu.VMEM((N, N), jnp.bfloat16), pltpu.VMEM((N, N), jnp.bfloat16)],
        compiler_params=LIMIT,
        cost_estimate=pl.CostEstimate(
            flops=8 * N**3, bytes_accessed=14 * N * N, transcendentals=3 * N * N
        ),
    )(feats, head_t, pose, pose_unit, pose_norm, target)


def local(pose_feats, text_feats, match, pose_head, text_head):
    batch_size = ROWS * 256
    logit_scale = 2.0 * math.sqrt(N)
    grad_scale = logit_scale / math.sqrt(batch_size)
    x = lax.axis_index("x")
    yl = lax.axis_index("yl")
    yh = lax.axis_index("yh")
    core = lax.axis_index("core")
    y = yh * 2 + yl
    first = core == 0

    text_group = lax.all_gather(text_feats, LINE, axis=0, tiled=True)
    ids = jnp.stack([match // 128, match % 128], axis=1).astype(jnp.bfloat16)
    shard = jnp.concatenate([pose_feats, jnp.pad(ids, ((0, 0), (0, EXTRA - 2)))], axis=1)
    pose_group = ring_gather(
        ring_gather(shard, True, jnp.where(first, x, y)), False, jnp.where(first, y, x)
    )
    pose_head_t = pose_head.T
    text_head_t = text_head.T

    pose, pose_unit, pose_norm = project(pose_group, pose_head_t)
    lanes = lax.broadcasted_iota(jnp.int32, (8, EXTRA), 1)
    pick = jnp.where(lanes == 0, 128.0, jnp.where(lanes == 1, 1.0, 0.0)).astype(jnp.bfloat16)
    group_ids = lax.dot_general(
        pick, pose_group[:, N:], NT, preferred_element_type=jnp.float32
    ).astype(jnp.int32)
    offset = group_ids - ((x * 2 + yl) * 2048 + yh * 512)
    inside = (offset >= 0) & (offset < 2048) & (offset % 1024 < 512)
    target = jnp.where(inside, offset // 1024 * 512 + offset % 1024, -1)

    loss_part, pose_part, text_part = score(
        logit_scale, grad_scale, text_group, text_head_t, pose, pose_unit, pose_norm, target
    )

    halves = text_part.reshape(2, N // 2, N)
    keep = lax.dynamic_index_in_dim(halves, core, 0, keepdims=False)
    give = lax.dynamic_index_in_dim(halves, 1 - core, 0, keepdims=False)
    got = swap_cores(give)
    text_sum = (keep.astype(jnp.float32) + got.astype(jnp.float32)).astype(jnp.bfloat16)
    text_back = lax.psum_scatter(text_sum, "z", scatter_dimension=0, tiled=True)

    parts = lax.all_to_all(pose_part.reshape(16, ROWS, N), PLANE, 0, 0)
    pose_back = jnp.sum(parts.astype(jnp.float32), axis=0).astype(jnp.bfloat16)

    pose_term = jnp.dot(pose_back, pose_group[:, :N], preferred_element_type=jnp.float32)
    text_term = jnp.dot(text_back, text_group, preferred_element_type=jnp.float32)

    pose_blocks = pose_term.reshape(ROWS, 8, 2, ROWS).transpose(2, 1, 0, 3).reshape(16, ROWS, ROWS)
    text_rows = text_back.astype(jnp.float32).reshape(ROWS, 16, ROWS).transpose(1, 0, 2)
    loss_rows = jnp.zeros((16, 8, 2 * ROWS), jnp.float32) + jnp.sum(loss_part)
    line = lax.all_to_all(
        jnp.concatenate([jnp.concatenate([pose_blocks, text_rows], axis=2), loss_rows], axis=1),
        LINE,
        0,
        0,
    )
    pose_sum = jnp.sum(line[:, :ROWS, :ROWS], axis=0)
    text_cols = line[:, :ROWS, ROWS:].reshape(N, ROWS).astype(jnp.bfloat16)
    loss_line = jnp.sum(line[:, ROWS, 0])

    text_blocks = text_term.reshape(ROWS, 16, ROWS).transpose(1, 0, 2)
    by_slot = pose_back.astype(jnp.float32).reshape(ROWS, 4, 4, ROWS)
    by_xy = jnp.where(first, by_slot.transpose(2, 1, 0, 3), by_slot.transpose(1, 2, 0, 3))
    pose_rows = (
        by_xy.reshape(4, 2, 2, ROWS, ROWS).transpose(0, 2, 1, 3, 4).reshape(16, ROWS, ROWS)
    )
    loss_rows = jnp.zeros((16, 8, 2 * ROWS), jnp.float32) + loss_line
    plane = lax.all_to_all(
        jnp.concatenate([jnp.concatenate([text_blocks, pose_rows], axis=2), loss_rows], axis=1),
        PLANE,
        0,
        0,
    )
    text_sum = jnp.sum(plane[:, :ROWS, :ROWS], axis=0)
    pose_cols = plane[:, :ROWS, ROWS:].reshape(N, ROWS).astype(jnp.bfloat16)
    loss = jnp.sum(plane[:, ROWS, 0]) / (batch_size * batch_size)

    grad_text = lax.dot_general(text_cols, text_head_t, TN, preferred_element_type=jnp.float32)
    grad_pose = lax.dot_general(pose_cols, pose_head_t, TN, preferred_element_type=jnp.float32)

    pose_mine = send(
        pose_sum.T, lambda x, y, z, c: (z // 2, y // 2 * 2 + z % 2, x * 2 + y % 2, c)
    )
    text_mine = send(text_sum.T, lambda x, y, z, c: (x, c * 2 + y % 2, z, y // 2))
    mine = jnp.concatenate([pose_mine, text_mine], axis=1)
    every = lax.all_to_all(jnp.broadcast_to(mine[None], (16, ROWS, 2 * ROWS)), NARROW, 0, 0)
    pose_cat = (
        every[:, :, :ROWS].reshape(2, 8, ROWS, ROWS).transpose(2, 1, 0, 3).reshape(ROWS, N)
    )
    text_cat = every[:, :, ROWS:].transpose(1, 0, 2).reshape(ROWS, N)
    return (loss, grad_pose, grad_text, jnp.concatenate([pose_cat, text_cat], axis=1))


def solution(mesh):
    fine = Mesh(mesh.devices.reshape(NX, 2, NC, 2, NZ), AXES)
    placed = (P(AXES, None), P(AXES, None), P(AXES), P(), P())
    return jax.shard_map(
        local,
        mesh=fine,
        in_specs=placed,
        out_specs=(P(), P(AXES, None), P(AXES, None), P(("x", "yl", "core"), None)),
        check_vma=False,
    )
```

time: 867 us -> 221 us (0.25)
  waiting for transfers between devices: 541 us -> 75.4 us
  matrix products: 159 us -> 7.3 us
  blocking collectives: 98.3 us -> 0 us
  starting transfers between devices: 1.03 us -> 47 us
  Pallas kernels: 0 us -> 32 us
  loops' own time: 26.5 us -> 0 us
  local copies, waits for them, and re-layouts: 15.5 us -> 26.6 us
    reduce_scatter x1, waiting for transfers between devices: 194 us -> 3.19 us  [local(): text_back = lax.psum_scatter(text_sum, 'z', scatter_dimension=0, tiled=True)]
    psum x1 -> x0, waiting for transfers between devices: 157 us -> none  [local(): head_grads = lax.psum(head_part, 'narrow')]
    dot_general x54 -> x5, matrix products: 159 us -> 7.3 us  [the longest x1 3.07 us: local(): lax.dot_general(pose_cols, pose_head_t, TN, preferred_element_type=jnp.fl...]
    ppermute x31 -> x11, waiting for transfers between devices: 105 us -> 12.3 us  [send(): return lax.ppermute(value, AXES, pairs_of(move))]
    psum x1 -> x0, blocking collectives: 78.3 us -> none  [local(): loss_all = lax.psum(loss_total, ('wide', 'narrow'))]
    all_gather x1, waiting for transfers between devices: 65.9 us -> 0.02 us  [local(): text_group = lax.all_gather(text_feats, LINE, axis=0, tiled=True)]
    all_to_all x0 -> x4, waiting for transfers between devices: none -> 59.2 us  [the longest x1 28.5 us: local(): parts = lax.all_to_all(pose_part.reshape(16, ROWS, N), PLANE, 0, 0)]
    pallas_call x0 -> x2, Pallas kernels: none -> 32 us  [the longest x1 24.3 us: score(): pl.pallas_call(functools.partial(pair_kernel, scale, grad_scale), out_sha...]
  transfers between devices with their start and end apart: 35 -> 17, of which waited for: 20 -> 9; matrix products, arithmetic and copies ran while one was open for 15% -> 16% of each run, Pallas kernels for 0% -> 4%
where the time goes in v1:
time: 221 us; the launch traced here: 219 us
  waiting for transfers between devices  75.4 us (34%)
  starting transfers between devices  47 us (21%)
  Pallas kernels  32 us (14%)
  local copies, waits for them, and re-layouts  26.6 us (12%)
  between operations  16.2 us (7%)
  other arithmetic  14.4 us (7%)
  matrix products  7.3 us (3%)
    all_to_all x1, waiting for transfers between devices, local(): parts = lax.all_to_all(pose_part.reshape(16, ROWS, N), PLANE, 0, 0)  28.5 us
    pallas_call x1, Pallas kernels, score(): pl.pallas_call(functools.partial(pair_kernel, scale, grad_scale), out_sha...  24.3 us
    ppermute x11, starting transfers between devices, send(): return lax.ppermute(value, AXES, pairs_of(move))  17 us
    all_to_all x1, waiting for transfers between devices, local(): lax.all_to_all(jnp.concatenate([jnp.concatenate([pose_blocks, text_rows],...  15.3 us
    all_to_all x1, starting transfers between devices, local(): lax.all_to_all(jnp.broadcast_to(mine[None], (16, ROWS, 2 * ROWS)), NARROW...  12.8 us
    ppermute x11, waiting for transfers between devices, send(): return lax.ppermute(value, AXES, pairs_of(move))  12.3 us
    unnamed x14, local copies, waits for them, and re-layouts  11.8 us
    all_to_all x1, waiting for transfers between devices, local(): lax.all_to_all(jnp.concatenate([jnp.concatenate([text_blocks, pose_rows],...  8.7 us
  transfers between devices with their start and end apart: 17, of which 9 were waited for; matrix products, arithmetic and copies ran while one was open for 16% of the time, Pallas kernels for 4%

profile of v1, /device:TPU:32, one launch (start us, length us, event | category | flops | bytes accessed | tf_op | source)
XLA Modules:
  0.0 218.9 jit_solution(11431154381559815766)
XLA Ops:
  7.2 0.7 all-gather.2.cloned.1.call-update
  7.9 0.7 convert_bitcast_fusion
  8.8 0.9 fusion.7
  9.7 1.6 collective-permute-start
  11.3 1.7 collective-permute-start.1
  13.0 3.1 %collective-permute-done = bf16[64,1152]{1,0:T(8,128)(2,1)S(1)} collective-permute-done((bf16[64,1152]{1,0:T(8,128)(2,1)S(1)}, bf16[64,1152]{1,0:T(8,128)(2,1)S(1)}, u32[]{:S(2)}, u32[]{:S(2)}) %collective-permute-start) | collective-permute-done | bytes 147488 | tf_op jit(solution)/shard_map/ppermute | solution.py:48
  16.2 0.3 collective-permute-start.2
  16.5 3.0 %collective-permute-start.3 = (bf16[32,1152]{1,0:T(8,128)(2,1)S(1)}, bf16[32,1152]{1,0:T(8,128)(2,1)S(1)}, u32[]{:S(2)}, u32[]{:S(2)}) collective-permute-start(bf16[32,1152]{1,0:T(8,128)(2,1)S(1)} %slice.59), channel_id=1, source_target_pairs={{0,192},{16,56},{1,193},{17,57},{2,194},{18,58},{3,195},{19,59},{4... | collective-permute-start | bytes 221192 | tf_op jit(solution)/shard_map/ppermute | solution.py:48
  19.5 2.2 collective-permute-done.2
  21.8 3.1 %collective-permute-start.5 = (bf16[256,1152]{1,0:T(8,128)(2,1)S(1)}, bf16[256,1152]{1,0:T(8,128)(2,1)S(1)}, u32[]{:S(2)}, u32[]{:S(2)}) collective-permute-start(bf16[256,1152]{1,0:T(8,128)(2,1)S(1)} %constant_dynamic-update-slice_fusion.5), channel_id=1, source_target_pairs={{0,40},{16,208},{1,41},{17,209},{2,42},{18,210},{3,43},{19,211},{4... | collective-permute-start | bytes 1769480 | tf_op jit(solution)/shard_map/ppermute | solution.py:48
  24.9 2.9 %copy.68 = bf16[1024,1024]{0,1:T(8,128)(2,1)S(1)} copy(bf16[1024,1024]{1,0:T(8,128)(2,1)} %param.8) | data formatting | bytes 4194304 | tf_op args[3]
  27.7 4.0 %copy.66 = bf16[1024,1024]{0,1:T(8,128)(2,1)} copy(bf16[1024,1024]{1,0:T(8,128)(2,1)} %param.9) | data formatting | bytes 4194304 | tf_op args[4]
  31.7 0.2 broadcast_in_dim.26
  32.0 0.3 collective-permute-done.5
  32.3 3.8 %collective-permute-start.7 = (bf16[128,1152]{1,0:T(8,128)(2,1)S(1)}, bf16[128,1152]{1,0:T(8,128)(2,1)S(1)}, u32[]{:S(2)}, u32[]{:S(2)}) collective-permute-start(bf16[128,1152]{1,0:T(8,128)(2,1)S(1)} %slice.61), channel_id=1, source_target_pairs={{0,40},{16,208},{1,41},{17,209},{2,42},{18,210},{3,43},{19,211},{4... | collective-permute-start | bytes 884744 | tf_op jit(solution)/shard_map/ppermute | solution.py:48
  36.1 1.0 slice.60
  37.1 0.3 collective-permute-start.6
  37.3 1.1 constant_dynamic-update-slice_fusion.3
  38.5 6.7 %collective-permute-done.6 = bf16[128,1152]{1,0:T(8,128)(2,1)S(1)} collective-permute-done((bf16[128,1152]{1,0:T(8,128)(2,1)S(1)}, bf16[128,1152]{1,0:T(8,128)(2,1)S(1)}, u32[]{:S(2)}, u32[]{:S(2)}) %collective-permute-start.6) | collective-permute-done | bytes 294944 | tf_op jit(solution)/shard_map/ppermute | solution.py:48
  45.3 1.4 copy-done.2
  46.8 7.7 %shard_map.84 = (bf16[1024,1024]{1,0:T(8,128)(2,1)S(1)}, f32[1024,1024]{1,0:T(8,128)}, f32[8,1024]{1,0:T(8,128)S(1)}) custom-call(bf16[1024,1152]{1,0:T(8,128)(2,1)} %copy-done.2, bf16[1024,1024]{1,0:T(8,128)(2,1)S(1)} %bitcast.57), custom_call_target="tpu_custom_call" | custom-call | flops 2147483648 | bytes 12582912 | tf_op jit(solution)/shard_map/pallas_call | solution.py:164
  54.5 1.3 copy-done.1
  55.9 1.2 fusion.11.target_ref
  57.1 24.3 %shard_map.85 = (f32[8,1024]{1,0:T(8,128)S(1)}, bf16[1024,1024]{1,0:T(8,128)(2,1)S(1)}, bf16[1024,1024]{1,0:T(8,128)(2,1)S(1)}) custom-call(bf16[1024,1024]{1,0:T(8,128)(2,1)} %all-gather.2.cloned.1.call-done.feats_ref, bf16[1024,1024]{1,0:T(8,128)(2,1)} %bitcast.60, bf16[1024,1024]{1,0:T(8,128)(2,1)} %copy-done.1, ...), custom_call_target="tpu_custom_call" | custom-call | flops 8589934592 | bytes 14680064 | tf_op jit(solution)/shard_map/pallas_call | solution.py:179
  81.4 1.3 copy-done
  82.9 4.7 %all-to-all-start = ((bf16[16,64,1024]{2,1,0:T(8,128)(2,1)}), bf16[16,64,1024]{2,1,0:T(8,128)(2,1)}, u32[]{:S(2)}, u32[]{:S(2)}) async-start(bf16[16,64,1024]{2,1,0:T(8,128)(2,1)} %bitcast.58), calls=%async_computation.1 | async-start | bytes 4194304 | tf_op jit(solution)/shard_map/all_to_all | solution.py:237
  87.7 2.6 %fusion = bf16[512,1024]{1,0:T(8,128)(2,1)} fusion(bf16[512,1024]{1,0:T(8,128)(2,1)} %collective-permute-done.8, bf16[2,512,1024]{2,1,0:T(8,128)(2,1)S(1)} %bitcast.56, s32[]{:T(128)S(6)} %select_n.154), kind=kLoop, calls=%fused_computation.2 | loop fusion | flops 2097152 | bytes 3145732 | tf_op jit(solution)/shard_map/convert_element_type | solution.py:234
  90.3 3.1 %slice_bitcast_fusion = bf16[1024,1024]{0,1:T(8,128)(2,1)} fusion(bf16[1024,1152]{1,0:T(8,128)(2,1)} %copy-done.2), kind=kLoop, calls=%fused_computation | loop fusion | bytes 4194304 | tf_op jit(solution)/shard_map/dot_general | solution.py:240
  93.4 2.9 %copy.73 = bf16[1024,1024]{1,0:T(8,128)(2,1)S(1)} copy(bf16[1024,1024]{0,1:T(8,128)(2,1)} %slice_bitcast_fusion) | data formatting | bytes 4194304 | tf_op jit(solution)/shard_map/dot_general | solution.py:240
  96.3 0.6 reduce_sum.58
  96.9 28.5 %all-to-all-done = bf16[16,64,1024]{2,1,0:T(8,128)(2,1)} async-done(((bf16[16,64,1024]{2,1,0:T(8,128)(2,1)}), bf16[16,64,1024]{2,1,0:T(8,128)(2,1)}, u32[]{:S(2)}, u32[]{:S(2)}) %all-to-all-start) | async-done | bytes 2097184 | tf_op jit(solution)/shard_map/all_to_all | solution.py:237
  125.4 2.0 reduce_sum.57
  127.4 1.1 convolution_bitcast_fusion
  128.6 3.2 %reduce-scatter.2.cloned.1.call-done = bf16[64,1024]{1,0:T(8,128)(2,1)} async-done(((bf16[512,1024]{1,0:T(8,128)(2,1)}), bf16[64,1024]{1,0:T(8,128)(2,1)}) %reduce-scatter.2.cloned.1.call-update) | async-done | bytes 131088 | tf_op jit(solution)/shard_map/reduce_scatter | solution.py:235
  131.8 1.1 reshape.64
  132.8 0.2 copy.89
  133.0 1.7 fusion.4
  134.7 5.5 %all-to-all-start.1 = ((f32[16,72,128]{2,1,0:T(8,128)}), f32[16,72,128]{2,1,0:T(8,128)S(1)}, u32[]{:S(2)}, u32[]{:S(2)}) async-start(f32[16,72,128]{2,1,0:T(8,128)} %fusion.4), calls=%async_computation.2 | async-start | bytes 1179648 | tf_op jit(solution)/shard_map/all_to_all | solution.py:246
  140.2 0.3 reshape.63
  140.5 0.2 bitcast_select_fusion
  140.7 0.2 copy.71
  140.9 0.8 copy-done.4
  141.8 0.5 fusion.23
  142.6 15.3 %all-to-all-done.1 = f32[16,72,128]{2,1,0:T(8,128)S(1)} async-done(((f32[16,72,128]{2,1,0:T(8,128)}), f32[16,72,128]{2,1,0:T(8,128)S(1)}, u32[]{:S(2)}, u32[]{:S(2)}) %all-to-all-start.1) | async-done | bytes 589856 | tf_op jit(solution)/shard_map/all_to_all | solution.py:246
  157.9 0.6 slice_reduce_fusion.3
  158.5 1.7 select_maximum_fusion
  160.1 6.9 %all-to-all-start.2 = ((f32[16,72,128]{2,1,0:T(8,128)}), f32[16,72,128]{2,1,0:T(8,128)}, u32[]{:S(2)}, u32[]{:S(2)}) async-start(f32[16,72,128]{2,1,0:T(8,128)} %select_maximum_fusion), calls=%async_computation.3 | async-start | bytes 1179648 | tf_op jit(solution)/shard_map/all_to_all | solution.py:263
  167.1 2.5 %collective-permute-start.9 = (f32[64,64]{0,1:T(8,128)S(1)}, f32[64,64]{0,1:T(8,128)S(1)}, u32[]{:S(2)}, u32[]{:S(2)}) collective-permute-start(f32[64,64]{0,1:T(8,128)S(1)} %bitcast.70), channel_id=1, source_target_pairs={{0,0},{16,16},{1,32},{17,48},{2,64},{18,80},{3,96},{19,112},{4,128... | collective-permute-start | bytes 49160 | tf_op jit(solution)/shard_map/ppermute | solution.py:48
  169.6 8.7 %all-to-all-done.2 = f32[16,72,128]{2,1,0:T(8,128)} async-done(((f32[16,72,128]{2,1,0:T(8,128)}), f32[16,72,128]{2,1,0:T(8,128)}, u32[]{:S(2)}, u32[]{:S(2)}) %all-to-all-start.2) | async-done | bytes 589856 | tf_op jit(solution)/shard_map/all_to_all | solution.py:263
  178.3 1.1 slice_reduce_fusion
  179.4 0.7 collective-permute-start.10
  180.2 0.9 broadcast_in_dim.31
  181.1 12.8 %all-to-all-start.3 = ((f32[16,64,128]{2,1,0:T(8,128)}), f32[16,64,128]{2,1,0:T(8,128)S(1)}, u32[]{:S(2)}, u32[]{:S(2)}) async-start(f32[16,64,128]{2,1,0:T(8,128)} %broadcast_in_dim.31), calls=%async_computation.4 | async-start | bytes 1048576 | tf_op jit(solution)/shard_map/all_to_all | solution.py:281
  194.0 1.5 fusion.25
  195.5 1.5 slice_reduce_fusion.2
  197.6 1.2 slice.85
  198.8 3.1 %fusion.24 = f32[64,1024]{1,0:T(8,128)} fusion(bf16[1024,64]{1,0:T(8,128)(2,1)S(1)} %bitcast.69, bf16[1024,1024]{1,0:T(8,128)(2,1)} %param.8), kind=kOutput, calls=%fused_computation.69 | convolution fusion | flops 134217728 | bytes 2490368 | tf_op jit(solution)/shard_map/dot_general | solution.py:274
  201.9 6.6 %all-to-all-done.3 = f32[16,64,128]{2,1,0:T(8,128)S(1)} async-done(((f32[16,64,128]{2,1,0:T(8,128)}), f32[16,64,128]{2,1,0:T(8,128)S(1)}, u32[]{:S(2)}, u32[]{:S(2)}) %all-to-all-start.3) | async-done | bytes 524320 | tf_op jit(solution)/shard_map/all_to_all | solution.py:281
  208.5 0.2 fusion.22
  208.7 0.4 copy.88
  209.1 0.5 reshape.60
  209.6 0.3 copy.80
  209.9 0.2 reshape.61
  210.1 0.8 pad_maximum_fusion
  (46 shorter events, 1.5 us)
Async XLA Ops:
  7.2 49.9 %all-gather.2.cloned.1.call-start = ((), (), s32[]{:S(2)}) async-start(), calls=%async_computation.5 | async-start | bytes 2228224 | tf_op jit(solution)/shard_map/all_gather | solution.py:207
  9.7 6.4 %collective-permute-start = (bf16[64,1152]{1,0:T(8,128)(2,1)S(1)}, bf16[64,1152]{1,0:T(8,128)(2,1)S(1)}, u32[]{:S(2)}, u32[]{:S(2)}) collective-permute-start(bf16[64,1152]{1,0:T(8,128)(2,1)S(1)} %get-tuple-element.18), channel_id=1, source_target_pairs={{0,64},{16,48},{1,65},{17,49},{2,66},{18,50},{3,67},{19,51},{4,68}... | collective-permute-start | bytes 442376 | tf_op jit(solution)/shard_map/ppermute | solution.py:48
  11.3 5.2 %collective-permute-start.1 = (bf16[64,1152]{1,0:T(8,128)(2,1)S(1)}, bf16[64,1152]{1,0:T(8,128)(2,1)S(1)}, u32[]{:S(2)}, u32[]{:S(2)}) collective-permute-start(bf16[64,1152]{1,0:T(8,128)(2,1)S(1)} %get-tuple-element.18), channel_id=1, source_target_pairs={{0,192},{16,56},{1,193},{17,57},{2,194},{18,58},{3,195},{19,59},{4... | collective-permute-start | bytes 442376 | tf_op jit(solution)/shard_map/ppermute | solution.py:48
  16.2 5.6 %collective-permute-start.2 = (bf16[32,1152]{1,0:T(8,128)(2,1)S(1)}, bf16[32,1152]{1,0:T(8,128)(2,1)S(1)}, u32[]{:S(2)}, u32[]{:S(2)}) collective-permute-start(bf16[32,1152]{1,0:T(8,128)(2,1)S(1)} %slice.58), channel_id=1, source_target_pairs={{0,64},{16,48},{1,65},{17,49},{2,66},{18,50},{3,67},{19,51},{4,68}... | collective-permute-start | bytes 221192 | tf_op jit(solution)/shard_map/ppermute | solution.py:48
  16.5 5.3 %collective-permute-start.3 = (bf16[32,1152]{1,0:T(8,128)(2,1)S(1)}, bf16[32,1152]{1,0:T(8,128)(2,1)S(1)}, u32[]{:S(2)}, u32[]{:S(2)}) collective-permute-start(bf16[32,1152]{1,0:T(8,128)(2,1)S(1)} %slice.59), channel_id=1, source_target_pairs={{0,192},{16,56},{1,193},{17,57},{2,194},{18,58},{3,195},{19,59},{4... | collective-permute-start | bytes 221192 | tf_op jit(solution)/shard_map/ppermute | solution.py:48
  21.8 10.5 %collective-permute-start.5 = (bf16[256,1152]{1,0:T(8,128)(2,1)S(1)}, bf16[256,1152]{1,0:T(8,128)(2,1)S(1)}, u32[]{:S(2)}, u32[]{:S(2)}) collective-permute-start(bf16[256,1152]{1,0:T(8,128)(2,1)S(1)} %constant_dynamic-update-slice_fusion.5), channel_id=1, source_target_pairs={{0,40},{16,208},{1,41},{17,209},{2,42},{18,210},{3,43},{19,211},{4... | collective-permute-start | bytes 1769480 | tf_op jit(solution)/shard_map/ppermute | solution.py:48
  24.9 11.2 %collective-permute-start.4 = (bf16[256,1152]{1,0:T(8,128)(2,1)S(1)}, bf16[256,1152]{1,0:T(8,128)(2,1)}, u32[]{:S(2)}, u32[]{:S(2)}) collective-permute-start(bf16[256,1152]{1,0:T(8,128)(2,1)S(1)} %constant_dynamic-update-slice_fusion.5), channel_id=1, source_target_pairs={{0,32},{16,80},{1,33},{17,81},{2,34},{18,82},{3,35},{19,83},{4,36}... | collective-permute-start | bytes 1769480 | tf_op jit(solution)/shard_map/ppermute | solution.py:48
  32.3 13.0 %collective-permute-start.7 = (bf16[128,1152]{1,0:T(8,128)(2,1)S(1)}, bf16[128,1152]{1,0:T(8,128)(2,1)S(1)}, u32[]{:S(2)}, u32[]{:S(2)}) collective-permute-start(bf16[128,1152]{1,0:T(8,128)(2,1)S(1)} %slice.61), channel_id=1, source_target_pairs={{0,40},{16,208},{1,41},{17,209},{2,42},{18,210},{3,43},{19,211},{4... | collective-permute-start | bytes 884744 | tf_op jit(solution)/shard_map/ppermute | solution.py:48
  37.1 8.2 %collective-permute-start.6 = (bf16[128,1152]{1,0:T(8,128)(2,1)S(1)}, bf16[128,1152]{1,0:T(8,128)(2,1)S(1)}, u32[]{:S(2)}, u32[]{:S(2)}) collective-permute-start(bf16[128,1152]{1,0:T(8,128)(2,1)S(1)} %slice.60), channel_id=1, source_target_pairs={{0,32},{16,80},{1,33},{17,81},{2,34},{18,82},{3,35},{19,83},{4,36}... | collective-permute-start | bytes 884744 | tf_op jit(solution)/shard_map/ppermute | solution.py:48
  45.3 1.5 copy-start.2
  54.5 1.4 copy-start.1
  81.4 1.3 copy-start
  82.8 4.9 %collective-permute-start.8 = (bf16[512,1024]{1,0:T(8,128)(2,1)S(1)}, bf16[512,1024]{1,0:T(8,128)(2,1)}, u32[]{:S(2)}, u32[]{:S(2)}) collective-permute-start(bf16[512,1024]{1,0:T(8,128)(2,1)S(1)} %dynamic-slice_bitcast_fusion), channel_id=1, source_target_pairs={{0,16},{16,0},{1,17},{17,1},{2,18},{18,2},{3,19},{19,3},{4,20},{20... | collective-permute-start | bytes 3145736 | tf_op jit(solution)/shard_map/ppermute | solution.py:48
  82.9 42.6 %all-to-all-start = ((bf16[16,64,1024]{2,1,0:T(8,128)(2,1)}), bf16[16,64,1024]{2,1,0:T(8,128)(2,1)}, u32[]{:S(2)}, u32[]{:S(2)}) async-start(bf16[16,64,1024]{2,1,0:T(8,128)(2,1)} %bitcast.58), calls=%async_computation.1 | async-start | bytes 4194304 | tf_op jit(solution)/shard_map/all_to_all | solution.py:237
  87.6 44.2 %reduce-scatter.2.cloned.1.call-start = ((), (), s32[]{:S(2)}) async-start(), calls=%async_computation.6 | async-start | bytes 1179648 | tf_op jit(solution)/shard_map/reduce_scatter | solution.py:235
  134.7 23.2 %all-to-all-start.1 = ((f32[16,72,128]{2,1,0:T(8,128)}), f32[16,72,128]{2,1,0:T(8,128)S(1)}, u32[]{:S(2)}, u32[]{:S(2)}) async-start(f32[16,72,128]{2,1,0:T(8,128)} %fusion.4), calls=%async_computation.2 | async-start | bytes 1179648 | tf_op jit(solution)/shard_map/all_to_all | solution.py:246
  140.2 1.6 copy-start.4
  140.5 1.2 copy-start.5
  160.1 33.9 %copy-start.3 = (bf16[1024,1024]{1,0:T(8,128)(2,1)S(1)}, bf16[1024,1024]{1,0:T(8,128)(2,1)}, u32[]{:S(2)}) copy-start(bf16[1024,1024]{1,0:T(8,128)(2,1)} %param.9) | copy-start | bytes 6291460
  160.1 18.2 %all-to-all-start.2 = ((f32[16,72,128]{2,1,0:T(8,128)}), f32[16,72,128]{2,1,0:T(8,128)}, u32[]{:S(2)}, u32[]{:S(2)}) async-start(f32[16,72,128]{2,1,0:T(8,128)} %select_maximum_fusion), calls=%async_computation.3 | async-start | bytes 1179648 | tf_op jit(solution)/shard_map/all_to_all | solution.py:263
  167.1 13.0 %collective-permute-start.9 = (f32[64,64]{0,1:T(8,128)S(1)}, f32[64,64]{0,1:T(8,128)S(1)}, u32[]{:S(2)}, u32[]{:S(2)}) collective-permute-start(f32[64,64]{0,1:T(8,128)S(1)} %bitcast.70), channel_id=1, source_target_pairs={{0,0},{16,16},{1,32},{17,48},{2,64},{18,80},{3,96},{19,112},{4,128... | collective-permute-start | bytes 49160 | tf_op jit(solution)/shard_map/ppermute | solution.py:48
  179.4 0.7 collective-permute-start.10
  181.1 27.5 %all-to-all-start.3 = ((f32[16,64,128]{2,1,0:T(8,128)}), f32[16,64,128]{2,1,0:T(8,128)S(1)}, u32[]{:S(2)}, u32[]{:S(2)}) async-start(f32[16,64,128]{2,1,0:T(8,128)} %broadcast_in_dim.31), calls=%async_computation.4 | async-start | bytes 1048576 | tf_op jit(solution)/shard_map/all_to_all | solution.py:281
Sparse Core Ops, SparseCore 0:
  9.8 41.6 all-gather.1
  91.0 40.7 reduce-scatter.1
